TPU v7x, 32 devices: a whole 2x2x4 slice. The times are simulated.
32 devices in a mesh: groups: 2 (over y), tile: 16 (over z, x, core).
Axes of the slice: x: 2, y: 2, z: 4, core: 2. Of those that a mesh axis runs over, the one named last changes fastest.
Arguments:
- features: bfloat16 [64, 12288], P(None, ('groups', 'tile')), parts along dimension 1, may hold values from -6 to 6
- rulebook: int32 [27, 12288], P(None, ('groups', 'tile')), parts along dimension 1, may hold values from 0 to 640, as said below
- send_lists: int32 [2, 32], P(None, ('groups', 'tile')), parts along dimension 1, may hold values from 0 to 3, as said below
- weight_first: bfloat16 [64, 1728], replicated, may hold values from -0.375 to 0.375
- weight_second: bfloat16 [64, 1728], replicated, may hold values from -0.75 to 0.75
- cotangent: bfloat16 [64, 12288], P(None, ('groups', 'tile')), parts along dimension 1, may hold values from -6 to 6
Outputs:
- out_features: bfloat16 [64, 12288], P(None, ('groups', 'tile')), parts along dimension 1
- d_features: bfloat16 [64, 12288], P(None, ('groups', 'tile')), parts along dimension 1
- grad_first: float32 [128, 1728], P('groups'), parts along dimension 0
- grad_second: float32 [128, 1728], P('groups'), parts along dimension 0
There are 2 independent parts, one for each index of `groups`. A program takes and returns all parts, laid end to end along the dimension named above; an argument that names none is the same for every part. Nothing has to cross between parts.
Inputs may be any that keep to these rules, and one draw needn't show every extreme that they name: `rulebook`: A tile's rows are occupied cells of its box of 3 x 64 x 16 lattice cells, exactly 128 of them in each plane; tile t borders tile t - 1 below and t + 1 above along the first dimension. Offset k = 9 (a + 1) + 3 (b + 1) + (c + 1), with a, b, c in -1, 0, 1, names the occupied cell at that displacement, or 640 where that cell is empty or outside the detector; offset 27 // 2 names the row itself. If offset k of voxel v names voxel u, then offset 27 - 1 - k of u names v. Every halo row that is named lies in a listed block. `send_lists`: row 0 of a tile lists the distinct blocks of it that hold the cells of its lowest plane, row 1 those that hold the cells of its highest plane, 1 block each; the first tile lists nothing in row 0 and the last nothing in row 1, their entries being 3.
All inputs are finite; a program needn't handle non-finite values.
Results may differ from a plain program's by a relative error of at most 0.0042.
Values may be sent and summed in bfloat16 or wider, within the bound.
A program may use at most 64 MiB of HBM per device.

v0:
```python
import math

import jax
import jax.numpy as jnp
from jax import lax
from jax.sharding import PartitionSpec as P


def with_halo(block, sides, width):
    for axis, dim in sides:
        count = lax.axis_size(axis)
        forward = [(i, i + 1) for i in range(count - 1)]
        backward = [(target, source) for source, target in forward]
        low = lax.ppermute(
            lax.slice_in_dim(block, block.shape[dim] - width, None, axis=dim), axis, forward
        )
        high = lax.ppermute(lax.slice_in_dim(block, 0, width, axis=dim), axis, backward)
        block = jnp.concatenate([low, block, high], axis=dim)
    return block


def channel_major(weight):
    width = weight.shape[0]
    return weight.reshape(width, -1, width).transpose(0, 2, 1).reshape(width, -1)


def boundary_blocks(values, send_lists):
    width, rows = values.shape
    halo = send_lists.shape[1] * 128
    blocks = jnp.concatenate(
        [values.reshape(width, rows // 128, 128), jnp.zeros((width, 1, 128), values.dtype)], axis=1
    )
    lower = blocks[:, send_lists[0]].reshape(width, halo)
    upper = blocks[:, send_lists[1]].reshape(width, halo)
    return jnp.concatenate([lower, upper], axis=1)


def extended(values, received):
    width = values.shape[0]
    halo = received.shape[1] // 4
    return jnp.concatenate(
        [
            values,
            received[:, :halo],
            received[:, 3 * halo :],
            jnp.zeros((width, 128), values.dtype),
        ],
        axis=1,
    )


def share_rim(values, send_lists):
    halo = send_lists.shape[1] * 128
    received = with_halo(boundary_blocks(values, send_lists), (("tile", 1),), halo)
    return extended(values, received)


def gathered(table, rulebook, start, block):
    indices = rulebook[:, start : start + block]
    columns = table[:, indices]
    return columns.reshape(table.shape[0] * indices.shape[0], block)


def apply_conv(weight_major, table, rulebook, block):
    rows = rulebook.shape[1]
    pieces = [
        jnp.dot(
            weight_major,
            gathered(table, rulebook, start, block),
            preferred_element_type=jnp.float32,
        )
        for start in range(0, rows, block)
    ]
    return jnp.concatenate(pieces, axis=1)


def weight_grad(grads, table, rulebook, block):
    width, rows = grads.shape
    total = jnp.zeros((width, table.shape[0] * rulebook.shape[0]), jnp.float32)
    for start in range(0, rows, block):
        columns = gathered(table, rulebook, start, block)
        total = total + lax.dot_general(
            grads[:, start : start + block],
            columns,
            (((1,), (1,)), ((), ())),
            preferred_element_type=jnp.float32,
        )
    return total.reshape(width, width, -1).transpose(0, 2, 1).reshape(width, -1)


def transposed(weight, grads, rulebook, send_lists, block):
    width, rows = grads.shape
    halo = send_lists.shape[1] * 128
    received = with_halo(boundary_blocks(grads, send_lists), (("tile", 1),), halo)
    table = extended(grads, received)
    mirror = weight.reshape(width, -1, width).transpose(2, 0, 1).reshape(width, -1)
    result = apply_conv(mirror, table, rulebook[::-1], block)
    return result


def body(features, rulebook, send_lists, weight_first, weight_second, cotangent):
    width, rows = features.shape
    block = math.gcd(rows, 512)
    x_table = share_rim(features, send_lists)
    pre_first = apply_conv(channel_major(weight_first), x_table, rulebook, block)
    hidden = jax.nn.silu(pre_first).astype(jnp.bfloat16)
    h_table = share_rim(hidden, send_lists)
    second = apply_conv(channel_major(weight_second), h_table, rulebook, block)
    out_features = (second + features.astype(jnp.float32)).astype(jnp.bfloat16)
    scale = 1.0 / math.sqrt(rows * lax.axis_size("tile"))
    grad_second = weight_grad(cotangent, h_table, rulebook, block)
    d_hidden = transposed(weight_second, cotangent, rulebook, send_lists, block)
    sigma = jax.nn.sigmoid(pre_first)
    d_pre = (d_hidden * sigma * (1.0 + pre_first * (1.0 - sigma))).astype(jnp.bfloat16)
    grad_first = weight_grad(d_pre, x_table, rulebook, block)
    d_input = transposed(weight_first, d_pre, rulebook, send_lists, block)
    d_features = (cotangent.astype(jnp.float32) + d_input).astype(jnp.bfloat16)
    grad_second, grad_first = lax.psum((grad_second, grad_first), "tile")
    return (out_features, d_features, grad_first * scale, grad_second * scale)


def solution(mesh):
    placed = (
        P(None, ("groups", "tile")),
        P(None, ("groups", "tile")),
        P(None, ("groups", "tile")),
        P(),
        P(),
        P(None, ("groups", "tile")),
    )
    return jax.shard_map(
        body,
        mesh=mesh,
        in_specs=placed,
        out_specs=(
            P(None, ("groups", "tile")),
            P(None, ("groups", "tile")),
            P("groups", None),
            P("groups", None),
        ),
        check_vma=False,
    )
```

profile of v0, /device:TPU:0, one launch (start us, length us, event | category | flops | bytes accessed | tf_op | source)
XLA Modules:
  0.0 274.4 jit_solution(2894194336046067937)
XLA Ops:
  7.2 1.3 fusion.44
  11.1 0.8 reshape.103
  13.6 2.4 collective-permute-start
  16.1 1.3 collective-permute-start.1
  17.5 1.4 collective-permute-start.5
  19.1 5.8 %collective-permute-start.4 = (bf16[64,128]{0,1:T(8,128)(2,1)S(1)}, bf16[64,128]{0,1:T(8,128)(2,1)S(1)}, u32[]{:S(2)}, u32[]{:S(2)}) collective-permute-start(bf16[64,128]{0,1:T(8,128)(2,1)S(1)} %bitcast.209), channel_id=1, source_target_pairs={{0,1},{1,2},{2,3},{3,4},{4,5},{5,6},{6,7},{7,8},{8,9},{9,10},{10,1... | collective-permute-start | bytes 49160 | tf_op jit(solution)/shard_map/ppermute | solution.py:14
  25.7 0.7 copy-done.11
  29.8 7.1 %gather_fusion.2 = bf16[3456,64]{1,0:T(8,128)(2,1)S(1)} fusion(bf16[64,768]{0,1:T(8,128)(2,1)S(1)} %get-tuple-element.115, s32[4096]{0:T(1024)S(1)} %get-tuple-element.120), kind=kCustom, calls=%fused_computation.2 | custom fusion | bytes 898560 | tf_op jit(solution)/shard_map/gather | solution.py:60
  36.9 1.6 copy.50
  38.5 2.0 reshape.117
  40.5 8.1 %gather_fusion.1 = bf16[3456,64]{1,0:T(8,128)(2,1)} fusion(bf16[64,768]{0,1:T(8,128)(2,1)S(1)} %get-tuple-element.115, s32[4096]{0:T(1024)S(1)} %get-tuple-element.121), kind=kCustom, calls=%fused_computation.1 | custom fusion | bytes 898560 | tf_op jit(solution)/shard_map/gather | solution.py:60
  49.0 0.7 copy-done
  50.2 1.6 copy.47
  51.8 2.0 reshape.116
  53.8 7.1 %gather_fusion = bf16[3456,64]{1,0:T(8,128)(2,1)S(1)} fusion(bf16[64,768]{0,1:T(8,128)(2,1)S(1)} %get-tuple-element.115, s32[4096]{0:T(1024)S(1)} %pad_clamp_fusion.5), kind=kCustom, calls=%fused_computation | custom fusion | bytes 898560 | tf_op jit(solution)/shard_map/gather | solution.py:60
  60.9 1.0 fusion.13
  62.0 0.9 copy.44
  63.0 7.1 %gather_fusion.7 = bf16[3456,64]{1,0:T(8,128)(2,1)S(1)} fusion(bf16[64,768]{0,1:T(8,128)(2,1)S(1)} %get-tuple-element.114, s32[4096]{0:T(1024)S(1)} %pad_clamp_fusion.1), kind=kCustom, calls=%fused_computation.7 | custom fusion | bytes 898560 | tf_op jit(solution)/shard_map/gather | solution.py:60
  70.5 8.1 %gather_fusion.8 = bf16[3456,64]{1,0:T(8,128)(2,1)S(1)} fusion(bf16[64,768]{0,1:T(8,128)(2,1)S(1)} %get-tuple-element.114, s32[4096]{0:T(1024)} %pad_clamp_fusion), kind=kCustom, calls=%fused_computation.8 | custom fusion | bytes 898560 | tf_op jit(solution)/shard_map/gather | solution.py:60
  78.6 1.1 copy.73
  79.7 0.9 fusion.6
  80.7 0.9 fusion.4
  81.6 7.1 %gather_fusion.6 = bf16[3456,64]{1,0:T(8,128)(2,1)S(1)} fusion(bf16[64,768]{0,1:T(8,128)(2,1)S(1)} %get-tuple-element.114, s32[4096]{0:T(1024)S(1)} %pad_clamp_fusion.2), kind=kCustom, calls=%fused_computation.6 | custom fusion | bytes 898560 | tf_op jit(solution)/shard_map/gather | solution.py:60
  90.0 3.6 %collective-permute-start.6 = (bf16[64,128]{1,0:T(8,128)(2,1)S(1)}, bf16[64,128]{1,0:T(8,128)(2,1)S(1)}, u32[]{:S(2)}, u32[]{:S(2)}) collective-permute-start(bf16[64,128]{1,0:T(8,128)(2,1)S(1)} %get-tuple-element.102), channel_id=1, source_target_pairs={{0,1},{1,2},{2,3},{3,4},{4,5},{5,6},{6,7},{7,8},{8,9},{9,10},{10,1... | collective-permute-start | bytes 49160 | tf_op jit(solution)/shard_map/ppermute | solution.py:14
  93.6 1.3 collective-permute-start.7
  94.9 3.0 %collective-permute-start.2 = (bf16[64,128]{1,0:T(8,128)(2,1)S(1)}, bf16[64,128]{1,0:T(8,128)(2,1)S(1)}, u32[]{:S(2)}, u32[]{:S(2)}) collective-permute-start(bf16[64,128]{1,0:T(8,128)(2,1)S(1)} %get-tuple-element.110), channel_id=1, source_target_pairs={{0,1},{1,2},{2,3},{3,4},{4,5},{5,6},{6,7},{7,8},{8,9},{9,10},{10,1... | collective-permute-start | bytes 49160 | tf_op jit(solution)/shard_map/ppermute | solution.py:14
  98.0 1.5 collective-permute-start.3
  99.8 0.7 copy-done.7
  100.8 0.7 copy-done.6
  102.2 1.1 copy.85
  103.3 1.1 reshape.119
  105.2 8.1 %gather_fusion.5 = bf16[3456,64]{1,0:T(8,128)(2,1)} fusion(bf16[64,768]{0,1:T(8,128)(2,1)S(1)} %copy.53, s32[4096]{0:T(1024)S(1)} %copy-done.25), kind=kCustom, calls=%fused_computation.5 | custom fusion | bytes 898560 | tf_op jit(solution)/shard_map/gather | solution.py:60
  113.3 7.1 %gather_fusion.4 = bf16[3456,64]{1,0:T(8,128)(2,1)S(1)} fusion(bf16[64,768]{0,1:T(8,128)(2,1)S(1)} %copy.53, s32[4096]{0:T(1024)S(1)} %copy-done.23), kind=kCustom, calls=%fused_computation.4 | custom fusion | bytes 898560 | tf_op jit(solution)/shard_map/gather | solution.py:60
  120.4 7.1 %gather_fusion.3 = bf16[3456,64]{1,0:T(8,128)(2,1)S(1)} fusion(bf16[64,768]{0,1:T(8,128)(2,1)S(1)} %copy.53, s32[4096]{0:T(1024)S(1)} %copy-done.18), kind=kCustom, calls=%fused_computation.3 | custom fusion | bytes 898560 | tf_op jit(solution)/shard_map/gather | solution.py:60
  128.3 8.0 %gather_fusion.11 = bf16[3456,64]{1,0:T(8,128)(2,1)} fusion(bf16[64,768]{0,1:T(8,128)(2,1)S(1)} %copy.75, s32[4096]{0:T(1024)S(1)} %copy-done.19), kind=kCustom, calls=%fused_computation.11 | custom fusion | bytes 898560 | tf_op jit(solution)/shard_map/gather | solution.py:60
  136.3 8.1 %gather_fusion.10 = bf16[3456,64]{1,0:T(8,128)(2,1)} fusion(bf16[64,768]{0,1:T(8,128)(2,1)S(1)} %copy.75, s32[4096]{0:T(1024)S(1)} %copy-done.21), kind=kCustom, calls=%fused_computation.10 | custom fusion | bytes 898560 | tf_op jit(solution)/shard_map/gather | solution.py:60
  144.4 8.1 %gather_fusion.9 = bf16[3456,64]{1,0:T(8,128)(2,1)} fusion(bf16[64,768]{0,1:T(8,128)(2,1)S(1)} %copy.75, s32[4096]{0:T(1024)S(1)} %pad_clamp_fusion.2), kind=kCustom, calls=%fused_computation.9 | custom fusion | bytes 898560 | tf_op jit(solution)/shard_map/gather | solution.py:60
  152.4 1.9 copy.62
  154.3 0.9 reshape.122
  155.3 1.6 convolution_bitcast_fusion
  157.3 0.9 copy.58
  158.8 0.9 copy.54
  161.8 1.1 copy.87
  162.9 1.1 reshape.124
  164.4 0.8 copy-done.4
  168.6 96.3 %all-reduce.7.cloned.1.call-done = (f32[64,1728]{1,0:T(8,128)}, f32[64,1728]{1,0:T(8,128)}) async-done(((f32[64,1728]{1,0:T(8,128)}, f32[64,1728]{1,0:T(8,128)}), (f32[64,1728]{1,0:T(8,128)}, f32[64,1728]{1,0:T(8,128)})) %all-reduce.7.cloned.1.call-update) | async-done | bytes 884752 | tf_op jit(solution)/shard_map/psum | solution.py:118
  264.9 1.9 broadcast_multiply_fusion.1
  266.8 0.8 broadcast_multiply_fusion
  (125 shorter events, 17.2 us)
Async XLA Ops:
  7.2 257.7 %all-reduce.7.cloned.1.call-start = ((), (), s32[]{:S(2)}) async-start(), calls=%async_computation | async-start | bytes 1835008 | tf_op jit(solution)/shard_map/psum | solution.py:118
  11.1 0.8 copy-start.9
  13.6 15.6 %collective-permute-start = (bf16[64,128]{0,1:T(8,128)(2,1)S(1)}, bf16[64,128]{0,1:T(8,128)(2,1)S(1)}, u32[]{:S(2)}, u32[]{:S(2)}) collective-permute-start(bf16[64,128]{0,1:T(8,128)(2,1)S(1)} %bitcast.206), channel_id=1, source_target_pairs={{0,1},{1,2},{2,3},{3,4},{4,5},{5,6},{6,7},{7,8},{8,9},{9,10},{10,1... | collective-permute-start | bytes 49160 | tf_op jit(solution)/shard_map/ppermute | solution.py:14
  16.1 13.1 %collective-permute-start.1 = (bf16[64,128]{0,1:T(8,128)(2,1)S(1)}, bf16[64,128]{0,1:T(8,128)(2,1)S(1)}, u32[]{:S(2)}, u32[]{:S(2)}) collective-permute-start(bf16[64,128]{0,1:T(8,128)(2,1)S(1)} %bitcast.207), channel_id=1, source_target_pairs={{1,0},{2,1},{3,2},{4,3},{5,4},{6,5},{7,6},{8,7},{9,8},{10,9},{11,1... | collective-permute-start | bytes 49160 | tf_op jit(solution)/shard_map/ppermute | solution.py:17
  17.5 7.3 %copy-start.26 = (s32[27,384]{1,0:T(8,128)S(1)}, s32[27,384]{1,0:T(8,128)}, u32[]{:S(2)}) copy-start(s32[27,384]{1,0:T(8,128)} %param.7) | copy-start | bytes 124420
  17.5 11.7 %collective-permute-start.5 = (bf16[64,128]{0,1:T(8,128)(2,1)S(1)}, bf16[64,128]{0,1:T(8,128)(2,1)S(1)}, u32[]{:S(2)}, u32[]{:S(2)}) collective-permute-start(bf16[64,128]{0,1:T(8,128)(2,1)S(1)} %bitcast.208), channel_id=1, source_target_pairs={{1,0},{2,1},{3,2},{4,3},{5,4},{6,5},{7,6},{8,7},{9,8},{10,9},{11,1... | collective-permute-start | bytes 49160 | tf_op jit(solution)/shard_map/ppermute | solution.py:17
  19.1 10.1 %collective-permute-start.4 = (bf16[64,128]{0,1:T(8,128)(2,1)S(1)}, bf16[64,128]{0,1:T(8,128)(2,1)S(1)}, u32[]{:S(2)}, u32[]{:S(2)}) collective-permute-start(bf16[64,128]{0,1:T(8,128)(2,1)S(1)} %bitcast.209), channel_id=1, source_target_pairs={{0,1},{1,2},{2,3},{3,4},{4,5},{5,6},{6,7},{7,8},{8,9},{9,10},{10,1... | collective-permute-start | bytes 49160 | tf_op jit(solution)/shard_map/ppermute | solution.py:14
  25.0 28.8 %copy-start.17 = (s32[4096]{0:T(1024)}, s32[4096]{0:T(1024)S(1)}, u32[]{:S(2)}) copy-start(s32[4096]{0:T(1024)S(1)} %pad_clamp_fusion.5) | copy-start | bytes 49156
  25.6 0.8 copy-start.11
  25.6 1.0 copy-start.15
  25.7 4.1 %copy-start.24 = (s32[4096]{0:T(1024)}, s32[4096]{0:T(1024)S(1)}, u32[]{:S(2)}) copy-start(s32[4096]{0:T(1024)S(1)} %get-tuple-element.120) | copy-start | bytes 49156
  25.7 14.8 %copy-start.22 = (s32[4096]{0:T(1024)}, s32[4096]{0:T(1024)S(1)}, u32[]{:S(2)}) copy-start(s32[4096]{0:T(1024)S(1)} %get-tuple-element.121) | copy-start | bytes 49156
  26.4 36.6 %copy-start.20 = (s32[4096]{0:T(1024)}, s32[4096]{0:T(1024)S(1)}, u32[]{:S(2)}) copy-start(s32[4096]{0:T(1024)S(1)} %pad_clamp_fusion.1) | copy-start | bytes 49156
  27.2 0.9 copy-start.16
  29.2 0.6 copy-start.27
  48.6 1.2 copy-start
  49.0 1.2 copy-start.1
  79.7 1.0 copy-start.5
  89.1 0.8 copy-start.12
  89.1 0.8 copy-start.13
  89.1 0.8 copy-start.14
  90.0 14.4 %collective-permute-start.6 = (bf16[64,128]{1,0:T(8,128)(2,1)S(1)}, bf16[64,128]{1,0:T(8,128)(2,1)S(1)}, u32[]{:S(2)}, u32[]{:S(2)}) collective-permute-start(bf16[64,128]{1,0:T(8,128)(2,1)S(1)} %get-tuple-element.102), channel_id=1, source_target_pairs={{0,1},{1,2},{2,3},{3,4},{4,5},{5,6},{6,7},{7,8},{8,9},{9,10},{10,1... | collective-permute-start | bytes 49160 | tf_op jit(solution)/shard_map/ppermute | solution.py:14
  93.6 10.8 %collective-permute-start.7 = (bf16[64,128]{1,0:T(8,128)(2,1)S(1)}, bf16[64,128]{1,0:T(8,128)(2,1)S(1)}, u32[]{:S(2)}, u32[]{:S(2)}) collective-permute-start(bf16[64,128]{1,0:T(8,128)(2,1)S(1)} %get-tuple-element.103), channel_id=1, source_target_pairs={{1,0},{2,1},{3,2},{4,3},{5,4},{6,5},{7,6},{8,7},{9,8},{10,9},{11,1... | collective-permute-start | bytes 49160 | tf_op jit(solution)/shard_map/ppermute | solution.py:17
  94.9 9.5 %collective-permute-start.2 = (bf16[64,128]{1,0:T(8,128)(2,1)S(1)}, bf16[64,128]{1,0:T(8,128)(2,1)S(1)}, u32[]{:S(2)}, u32[]{:S(2)}) collective-permute-start(bf16[64,128]{1,0:T(8,128)(2,1)S(1)} %get-tuple-element.110), channel_id=1, source_target_pairs={{0,1},{1,2},{2,3},{3,4},{4,5},{5,6},{6,7},{7,8},{8,9},{9,10},{10,1... | collective-permute-start | bytes 49160 | tf_op jit(solution)/shard_map/ppermute | solution.py:14
  98.0 6.5 %collective-permute-start.3 = (bf16[64,128]{1,0:T(8,128)(2,1)S(1)}, bf16[64,128]{1,0:T(8,128)(2,1)S(1)}, u32[]{:S(2)}, u32[]{:S(2)}) collective-permute-start(bf16[64,128]{1,0:T(8,128)(2,1)S(1)} %get-tuple-element.111), channel_id=1, source_target_pairs={{1,0},{2,1},{3,2},{4,3},{5,4},{6,5},{7,6},{8,7},{9,8},{10,9},{11,1... | collective-permute-start | bytes 49160 | tf_op jit(solution)/shard_map/ppermute | solution.py:17
  99.5 1.0 copy-start.7
  100.5 1.0 copy-start.6
  103.3 1.1 copy-start.28
  104.5 0.7 copy-start.25
  105.2 8.1 %copy-start.23 = (s32[4096]{0:T(1024)S(1)}, s32[4096]{0:T(1024)}, u32[]{:S(2)}) copy-start(s32[4096]{0:T(1024)} %copy-done.22) | copy-start | bytes 49156
  113.3 7.1 %copy-start.18 = (s32[4096]{0:T(1024)S(1)}, s32[4096]{0:T(1024)}, u32[]{:S(2)}) copy-start(s32[4096]{0:T(1024)} %copy-done.17) | copy-start | bytes 49156
  127.6 0.7 copy-start.19
  128.3 8.0 %copy-start.21 = (s32[4096]{0:T(1024)S(1)}, s32[4096]{0:T(1024)}, u32[]{:S(2)}) copy-start(s32[4096]{0:T(1024)} %copy-done.20) | copy-start | bytes 49156
  160.1 1.0 copy-start.8
  162.9 1.2 copy-start.3
  164.0 1.2 copy-start.4
  165.5 1.2 copy-start.2
  264.9 1.9 copy-start.10
Sparse Core Ops, SparseCore 0:
  167.4 97.3 all-reduce.6
where the time goes:
time: 276 us; the launch traced here: 274 us
  local copies, waits for them, and re-layouts  125 us (45%)
  waiting for transfers between devices  96.3 us (35%)
  starting transfers between devices  20.3 us (7%)
  between operations  18.7 us (7%)
  matrix products  8.97 us (3%)
  other arithmetic  4.94 us (2%)
    gather x24, local copies, waits for them, and re-layouts, gathered(): columns = table[:, indices]  102 us
    psum x1, waiting for transfers between devices, body(): grad_second, grad_first = lax.psum((grad_second, grad_first), 'tile')  96.3 us
    ppermute x4, starting transfers between devices, with_halo(): lax.ppermute(lax.slice_in_dim(block, block.shape[dim] - width, None, axis...  14.8 us
    unnamed x60, local copies, waits for them, and re-layouts  7.86 us
    dot_general x12, matrix products, apply_conv(): jnp.dot(weight_major, gathered(table, rulebook, start, block), preferred_...  7.27 us
  transfers between devices with their start and end apart: 9, of which 1 were waited for; matrix products, arithmetic and copies ran while one was open for 3% of the time, Pallas kernels for 0%

commit v1 on v0

v1 whole, which is shorter than its diff:
```python
import functools
import math

import jax
import jax.numpy as jnp
from jax import lax
from jax.experimental import pallas as pl
from jax.experimental.pallas import tpu as pltpu
from jax.sharding import PartitionSpec as P

LANES = 128
BF = jnp.bfloat16
F32 = jnp.float32
TRANS_RHS = (((1,), (1,)), ((), ()))


def chunk_plan(width, cols, chips):
    row_parts = math.gcd(width // 16, chips)
    col_parts = chips // row_parts
    piece_cols = -(-cols // (col_parts * LANES)) * LANES
    return row_parts, col_parts, width // row_parts, piece_cols


def kernel(
    count, plan, scale,
    x_ref, rule_ref, lists_ref, w1_ref, w2_ref, cot_ref,
    out_ref, dx_ref, g1_ref, g2_ref,
    hot, gat_a, gat_b, mir1, mir2, own, hsend, halo, part, peer_in, rs_out, rs_in, ag,
    hs_sem, hr_sem, p_sem, rs_s, rs_r, ag_s, ag_r, fw_s, fw_r,
):
    width, rows = x_ref.shape
    offsets = rule_ref.shape[0]
    group = offsets // 3
    blocks = rows // LANES
    chips = count // 2
    row_parts, col_parts, piece_rows, piece_cols = plan
    missing = rows + 2 * LANES
    t = lax.axis_index("tile")
    core = lax.rem(t, 2)
    chip = t // 2
    peer = t + 1 - 2 * core

    def lanes(b):
        return slice(b * LANES, (b + 1) * LANES)

    def there(distance):
        return 2 * lax.rem(chip + distance, chips) + core

    barrier = pltpu.get_barrier_semaphore()
    beside = lax.rem(t + 2 * core - 1 + count, count)
    pl.semaphore_signal(barrier, inc=1, device_id={"tile": peer})
    pl.semaphore_signal(barrier, inc=1, device_id={"tile": beside})
    for d in range(1, chips):
        pl.semaphore_signal(barrier, inc=1, device_id={"tile": there(d)})

    def halo_copy(phase, up):
        return pltpu.make_async_remote_copy(
            src_ref=hsend.at[phase, up],
            dst_ref=halo.at[phase, 1 - up],
            send_sem=hs_sem.at[phase, up],
            recv_sem=hr_sem.at[phase, 1 - up],
            device_id={"tile": t + 2 * up - 1},
        )

    def pick_boundary(phase):
        for up in range(2):
            listed = jnp.broadcast_to(lists_ref[up : up + 1, :], (2 * width, LANES))
            chosen = jnp.zeros((2 * width, LANES), F32)
            for q in range(blocks):
                chosen = jnp.where(listed == q, own[phase, q], chosen)
            hsend[phase, up] = chosen.astype(BF)

    def send_halo(phase):
        @pl.when(t > 0)
        def _():
            halo_copy(phase, 0).start()

        @pl.when(t < count - 1)
        def _():
            halo_copy(phase, 1).start()

    def wait_halo(phase):
        @pl.when(t > 0)
        def _():
            halo_copy(phase, 1).wait_recv()

        @pl.when(t == 0)
        def _():
            halo[phase, 0] = jnp.zeros((2 * width, LANES), BF)

        @pl.when(t < count - 1)
        def _():
            halo_copy(phase, 0).wait_recv()

        @pl.when(t == count - 1)
        def _():
            halo[phase, 1] = jnp.zeros((2 * width, LANES), BF)

    def wait_sent(phase):
        @pl.when(t > 0)
        def _():
            halo_copy(phase, 0).wait_send()

        @pl.when(t < count - 1)
        def _():
            halo_copy(phase, 1).wait_send()

    for q in range(blocks):
        own[0, q] = jnp.concatenate([x_ref[:, lanes(q)], cot_ref[:, lanes(q)]], axis=0).astype(F32)
    pick_boundary(0)
    pl.semaphore_wait(barrier, chips + 1)
    send_halo(0)

    reach = jax.lax.broadcasted_iota(jnp.int32, (LANES, LANES), 0)
    firsts = {}
    for a in range(3):
        for b in range(blocks):
            base = b * LANES
            if a != 1:
                low = rule_ref[a * group : a * group + 1, lanes(b)]
                for j in range(1, group):
                    k = a * group + j
                    low = jnp.minimum(low, rule_ref[k : k + 1, lanes(b)])
                low = jnp.min(low, axis=1, keepdims=True)
                firsts[a, b] = low
                base = jnp.zeros_like(low)
                for q in range(1, blocks + 2):
                    base = jnp.where((low >= q * LANES) & (low < missing), q * LANES, base)
            for j in range(group):
                k = a * group + j
                row = rule_ref[k : k + 1, lanes(b)] - base
                hit = jnp.broadcast_to(row, (LANES, LANES)) == reach
                hot[a, b, :, lanes(j)] = jnp.where(hit, 1.0, 0.0).astype(BF)

    for w_ref, m_ref in ((w2_ref, mir2), (w1_ref, mir1)):
        for k in range(0, offsets, 2):
            last = min(k + 2, offsets)
            stack = [
                w_ref[:, (offsets - 1 - i) * width : (offsets - i) * width].astype(F32)
                for i in range(k, last)
            ]
            stack = jnp.concatenate(stack, axis=0) if len(stack) > 1 else stack[0]
            m_ref[:, k * width : last * width] = stack.T.astype(BF)

    def gather(phase, a, b):
        if a == 1:
            source = own[phase, b]
        else:
            low = jnp.broadcast_to(firsts[a, b], (2 * width, LANES))
            source = None
            for q in range(blocks):
                if q != b:
                    block = own[phase, q]
                    if source is None:
                        source = block
                    else:
                        source = jnp.where((low >= q * LANES) & (low < (q + 1) * LANES), block, source)
            rim = halo[phase, a // 2].astype(F32)
            source = jnp.where((low >= rows) & (low < missing), rim, source)
        source = source.astype(BF)
        for j in range(0, group, 2):
            last = min(j + 2, group)
            res = jnp.dot(
                source, hot[a, b, :, j * LANES : last * LANES], preferred_element_type=F32
            ).astype(BF)
            for i in range(j, last):
                k = a * group + i
                gat_a[k * width : (k + 1) * width, lanes(b)] = res[:width, lanes(i - j)]
                gat_b[k * width : (k + 1) * width, lanes(b)] = res[width:, lanes(i - j)]

    for b in range(blocks):
        gather(0, 1, b)
    wait_halo(0)
    for a in (0, 2):
        for b in range(blocks):
            gather(0, a, b)

    pre = jnp.dot(w1_ref[...], gat_a[...], preferred_element_type=F32)
    d_hidden = jnp.dot(mir2[...], gat_b[...], preferred_element_type=F32)
    sigma = 1.0 / (1.0 + jnp.exp(-pre))
    hidden = (pre * sigma).astype(BF)
    d_pre = (d_hidden * sigma * (1.0 + pre * (1.0 - sigma))).astype(BF)
    both = jnp.concatenate([hidden, d_pre], axis=0).astype(F32)
    for q in range(blocks):
        own[1, q] = both[:, lanes(q)]
    pick_boundary(1)
    send_halo(1)

    cols = offsets * width
    to_peer = pltpu.make_async_remote_copy(
        src_ref=part.at[1 - core],
        dst_ref=peer_in,
        send_sem=p_sem.at[0],
        recv_sem=p_sem.at[1],
        device_id={"tile": peer},
    )
    spare = part.shape[2] - cols
    if spare:
        for g in range(2):
            part[g, :, cols:] = jnp.zeros((width, spare), F32)
    part[0, :, :cols] = lax.dot_general(d_pre, gat_a[...], TRANS_RHS, preferred_element_type=F32)

    @pl.when(core == 1)
    def _():
        to_peer.start()

    for k in range(0, offsets, 2):
        last = min(k + 2, offsets)
        top = (offsets - k) * width
        terms = lax.dot_general(
            gat_b[(offsets - last) * width : top, :], hidden, TRANS_RHS, preferred_element_type=F32
        )
        pieces = [
            terms[(last - 1 - i) * width : (last - i) * width, :] for i in range(k, last)
        ]
        pieces = jnp.concatenate(pieces, axis=1) if len(pieces) > 1 else pieces[0]
        part[1, :, k * width : last * width] = pieces

    @pl.when(core == 0)
    def _():
        to_peer.start()

    for b in range(blocks):
        gather(1, 1, b)

    def piece(j):
        r, c = (j // col_parts) * piece_rows, (j % col_parts) * piece_cols
        return slice(r, r + piece_rows), slice(c, c + piece_cols)

    to_peer.wait_recv()
    for j in range(chips):
        r, c = piece(j)
        rs_out[j] = (part[core, r, c] + peer_in[r, c]).astype(BF)

    def rs_copy(d):
        target = lax.rem(chip + d, chips)
        return pltpu.make_async_remote_copy(
            src_ref=rs_out.at[target],
            dst_ref=rs_in.at[chip],
            send_sem=rs_s.at[target],
            recv_sem=rs_r.at[chip],
            device_id={"tile": 2 * target + core},
        )

    def rs_arrival(d):
        source = lax.rem(chip + d, chips)
        return source, pltpu.make_async_remote_copy(
            src_ref=rs_out.at[source],
            dst_ref=rs_in.at[source],
            send_sem=rs_s.at[source],
            recv_sem=rs_r.at[source],
            device_id={"tile": 2 * source + core},
        )

    for d in range(1, chips):
        rs_copy(d).start()

    wait_halo(1)
    for a in (0, 2):
        for b in range(blocks):
            gather(1, a, b)
    second = jnp.dot(w2_ref[...], gat_a[...], preferred_element_type=F32)
    out_ref[...] = (second + x_ref[...].astype(F32)).astype(BF)
    d_input = jnp.dot(mir1[...], gat_b[...], preferred_element_type=F32)
    dx_ref[...] = (cot_ref[...].astype(F32) + d_input).astype(BF)

    total = rs_out[chip].astype(F32)
    for d in range(1, chips):
        source, arrival = rs_arrival(d)
        arrival.wait_recv()
        total = total + rs_in[source].astype(F32)
    ag[core, chip] = (total * scale).astype(BF)

    def ag_copy(d):
        target = lax.rem(chip + d, chips)
        return pltpu.make_async_remote_copy(
            src_ref=ag.at[core, chip],
            dst_ref=ag.at[core, chip],
            send_sem=ag_s.at[target],
            recv_sem=ag_r.at[chip],
            device_id={"tile": 2 * target + core},
        )

    def ag_arrival(source):
        return pltpu.make_async_remote_copy(
            src_ref=ag.at[core, source],
            dst_ref=ag.at[core, source],
            send_sem=ag_s.at[source],
            recv_sem=ag_r.at[source],
            device_id={"tile": 2 * source + core},
        )

    def forward(source):
        return pltpu.make_async_remote_copy(
            src_ref=ag.at[core, source],
            dst_ref=ag.at[core, source],
            send_sem=fw_s.at[source],
            recv_sem=fw_r.at[source],
            device_id={"tile": peer},
        )

    def forwarded(source):
        return pltpu.make_async_remote_copy(
            src_ref=ag.at[1 - core, source],
            dst_ref=ag.at[1 - core, source],
            send_sem=fw_s.at[source],
            recv_sem=fw_r.at[source],
            device_id={"tile": peer},
        )

    for d in range(1, chips):
        ag_copy(d).start()
    forward(chip).start()
    for d in range(1, chips):
        source = lax.rem(chip + chips - d, chips)
        ag_arrival(source).wait_recv()
        forward(source).start()
    for j in range(chips):
        forwarded(j).wait_recv()
    for j in range(chips):
        r, c = piece(j)
        live = min(c.stop, cols) - c.start
        if live > 0:
            place = slice(c.start, c.start + live)
            g1_ref[r, place] = ag[0, j, :, :live].astype(F32)
            g2_ref[r, place] = ag[1, j, :, :live].astype(F32)

    wait_sent(0)
    wait_sent(1)
    to_peer.wait_send()
    for d in range(1, chips):
        rs_copy(d).wait_send()
        ag_copy(d).wait_send()
    for j in range(chips):
        forward(j).wait_send()


def body(count, features, rulebook, send_lists, weight_first, weight_second, cotangent):
    width, rows = features.shape
    offsets = rulebook.shape[0]
    cols = offsets * width
    blocks = rows // LANES
    chips = count // 2
    plan = chunk_plan(width, cols, chips)
    row_parts, col_parts, piece_rows, piece_cols = plan
    scale = 1.0 / math.sqrt(rows * count)
    dma = pltpu.SemaphoreType.DMA
    vmem = pl.BlockSpec(memory_space=pltpu.VMEM)
    return pl.pallas_call(
        functools.partial(kernel, count, plan, scale),
        out_shape=(
            jax.ShapeDtypeStruct((width, rows), BF),
            jax.ShapeDtypeStruct((width, rows), BF),
            jax.ShapeDtypeStruct((width, cols), F32),
            jax.ShapeDtypeStruct((width, cols), F32),
        ),
        in_specs=[vmem] * 6,
        out_specs=(vmem,) * 4,
        scratch_shapes=[
            pltpu.VMEM((3, blocks, LANES, offsets // 3 * LANES), BF),
            pltpu.VMEM((cols, rows), BF),
            pltpu.VMEM((cols, rows), BF),
            pltpu.VMEM((width, cols), BF),
            pltpu.VMEM((width, cols), BF),
            pltpu.VMEM((2, blocks, 2 * width, LANES), F32),
            pltpu.VMEM((2, 2, 2 * width, LANES), BF),
            pltpu.VMEM((2, 2, 2 * width, LANES), BF),
            pltpu.VMEM((2, width, col_parts * piece_cols), F32),
            pltpu.VMEM((width, col_parts * piece_cols), F32),
            pltpu.VMEM((chips, piece_rows, piece_cols), BF),
            pltpu.VMEM((chips, piece_rows, piece_cols), BF),
            pltpu.VMEM((2, chips, piece_rows, piece_cols), BF),
            dma((2, 2)),
            dma((2, 2)),
            dma((2,)),
            dma((chips,)),
            dma((chips,)),
            dma((chips,)),
            dma((chips,)),
            dma((chips,)),
            dma((chips,)),
        ],
        compiler_params=pltpu.CompilerParams(
            collective_id=0, has_side_effects=True, vmem_limit_bytes=40 * 1024 * 1024
        ),
    )(features, rulebook, send_lists, weight_first, weight_second, cotangent)


def solution(mesh):
    split = P(None, ("groups", "tile"))
    return jax.shard_map(
        functools.partial(body, mesh.shape["tile"]),
        mesh=mesh,
        in_specs=(split, split, split, P(), P(), split),
        out_specs=(split, split, P("groups", None), P("groups", None)),
        check_vma=False,
    )
```

time: 276 us -> 34 us (0.12)
  local copies, waits for them, and re-layouts: 125 us -> 7.79 us
  waiting for transfers between devices: 96.3 us -> 0 us
  Pallas kernels: 0 us -> 25.2 us
  starting transfers between devices: 20.3 us -> 0 us
  between operations: 18.7 us -> 0.65 us
  matrix products: 8.97 us -> 0 us
  other arithmetic: 4.94 us -> 0 us
    gather x24 -> x0, local copies, waits for them, and re-layouts: 102 us -> none  [gathered(): columns = table[:, indices]]
    psum x1 -> x0, waiting for transfers between devices: 96.3 us -> none  [body(): grad_second, grad_first = lax.psum((grad_second, grad_first), 'tile')]
    pallas_call x0 -> x1, Pallas kernels: none -> 25.2 us  [body(): pl.pallas_call(functools.partial(kernel, count, plan, scale), out_shape=(...]
    ppermute x8 -> x0, starting transfers between devices: 20.3 us -> none  [the longest x4 14.8 us: with_halo(): lax.ppermute(lax.slice_in_dim(block, block.shape[dim] - width, None, axis...]
    reshape x16 -> x0, local copies, waits for them, and re-layouts: 9.49 us -> none  [the longest x6 5.29 us: gathered(): return columns.reshape(table.shape[0] * indices.shape[0], block)]
    dot_general x18 -> x0, matrix products: 8.97 us -> none  [the longest x12 7.27 us: apply_conv(): jnp.dot(weight_major, gathered(table, rulebook, start, block), preferred_...]
    transpose x4 -> x0, local copies, waits for them, and re-layouts: 3.24 us -> none  [the longest x2 2.15 us: weight_grad(): return total.reshape(width, width, -1).transpose(0, 2, 1).reshape(width, -1)]
    unnamed x60 -> x15, local copies, waits for them, and re-layouts: 7.86 us -> 7.79 us
  transfers between devices with their start and end apart: 9 -> 0, of which waited for: 1 -> 0; matrix products, arithmetic and copies ran while one was open for 3% -> 0% of each run, Pallas kernels for 0% -> 0%
where the time goes in v1:
time: 34 us; the launch traced here: 33.6 us
  Pallas kernels  25.2 us (74%)
  local copies, waits for them, and re-layouts  7.79 us (23%)
  between operations  0.65 us (2%)
    pallas_call x1, Pallas kernels, body(): pl.pallas_call(functools.partial(kernel, count, plan, scale), out_shape=(...  25.2 us
    unnamed x15, local copies, waits for them, and re-layouts  7.79 us

profile of v1, /device:TPU:0, one launch (start us, length us, event | category | flops | bytes accessed | tf_op | source)
XLA Modules:
  0.0 33.6 jit_solution(9441432454566617629)
XLA Ops:
  0.6 0.7 %copy.10.lists_ref = s32[2,1]{1,0:T(2,128)S(1)} copy(s32[2,1]{0,1:T(1,128)} %param.8) | data formatting | bytes 16 | tf_op args[2]
  1.4 0.0 copy-start
  1.4 0.9 %copy-done = bf16[64,1728]{1,0:T(8,128)(2,1)S(1)} copy-done((bf16[64,1728]{1,0:T(8,128)(2,1)S(1)}, bf16[64,1728]{1,0:T(8,128)(2,1)}, u32[]{:S(2)}) %copy-start) | copy-done | bytes 221208
  2.3 0.0 copy-start.1
  2.3 0.9 %copy-done.1 = bf16[64,1728]{1,0:T(8,128)(2,1)S(1)} copy-done((bf16[64,1728]{1,0:T(8,128)(2,1)S(1)}, bf16[64,1728]{1,0:T(8,128)(2,1)}, u32[]{:S(2)}) %copy-start.1) | copy-done | bytes 221208
  3.3 0.0 copy-start.2
  3.3 0.8 %copy-done.2 = bf16[64,384]{1,0:T(8,128)(2,1)S(1)} copy-done((bf16[64,384]{1,0:T(8,128)(2,1)S(1)}, bf16[64,384]{1,0:T(8,128)(2,1)}, u32[]{:S(2)}) %copy-start.2) | copy-done | bytes 49176
  4.0 0.0 copy-start.3
  4.1 0.8 %copy-done.3 = s32[27,384]{1,0:T(8,128)S(1)} copy-done((s32[27,384]{1,0:T(8,128)S(1)}, s32[27,384]{1,0:T(8,128)}, u32[]{:S(2)}) %copy-start.3) | copy-done | bytes 41496
  4.8 0.0 copy-start.4
  4.9 0.8 %copy-done.4 = bf16[64,384]{1,0:T(8,128)(2,1)S(1)} copy-done((bf16[64,384]{1,0:T(8,128)(2,1)S(1)}, bf16[64,384]{1,0:T(8,128)(2,1)}, u32[]{:S(2)}) %copy-start.4) | copy-done | bytes 49176
  5.6 25.2 %shard_map.93 = (bf16[64,384]{1,0:T(8,128)(2,1)S(1)}, bf16[64,384]{1,0:T(8,128)(2,1)S(1)}, f32[64,1728]{1,0:T(8,128)S(1)}, f32[64,1728]{1,0:T(8,128)S(1)}) custom-call(bf16[64,384]{1,0:T(8,128)(2,1)S(1)} %copy-done.2, s32[27,384]{1,0:T(8,128)S(1)} %copy-done.3, s32[2,1]{1,0:T(2,128)S(1)} %copy.10.lists_ref, bf16[64,1728]{1,0:T(8,128)(2,1)S(1)} %copy-done, ...), custom_call_target="tpu_custom_call" | custom-call | tf_op jit(solution)/shard_map/pallas_call | solution.py:349
  30.8 0.6 %copy.15 = bf16[64,384]{1,0:T(8,128)(2,1)} copy(bf16[64,384]{1,0:T(8,128)(2,1)S(1)} %get-tuple-element.8) | data formatting | bytes 98304
  31.5 0.6 %copy.16 = bf16[64,384]{1,0:T(8,128)(2,1)} copy(bf16[64,384]{1,0:T(8,128)(2,1)S(1)} %get-tuple-element.9) | data formatting | bytes 98304
  32.1 0.8 %copy.17 = f32[64,1728]{1,0:T(8,128)} copy(f32[64,1728]{1,0:T(8,128)S(1)} %get-tuple-element.10) | data formatting | bytes 884736
  32.9 0.8 %copy.18 = f32[64,1728]{1,0:T(8,128)} copy(f32[64,1728]{1,0:T(8,128)S(1)} %get-tuple-element.11) | data formatting | bytes 884736
Async XLA Ops:
  1.4 0.9 %copy-start = (bf16[64,1728]{1,0:T(8,128)(2,1)S(1)}, bf16[64,1728]{1,0:T(8,128)(2,1)}, u32[]{:S(2)}) copy-start(bf16[64,1728]{1,0:T(8,128)(2,1)} %w1_ref.1) | copy-start | bytes 663556
  2.3 0.9 %copy-start.1 = (bf16[64,1728]{1,0:T(8,128)(2,1)S(1)}, bf16[64,1728]{1,0:T(8,128)(2,1)}, u32[]{:S(2)}) copy-start(bf16[64,1728]{1,0:T(8,128)(2,1)} %w2_ref.1) | copy-start | bytes 663556
  3.3 0.8 %copy-start.2 = (bf16[64,384]{1,0:T(8,128)(2,1)S(1)}, bf16[64,384]{1,0:T(8,128)(2,1)}, u32[]{:S(2)}) copy-start(bf16[64,384]{1,0:T(8,128)(2,1)} %x_ref.1) | copy-start | bytes 147460
  4.0 0.8 %copy-start.3 = (s32[27,384]{1,0:T(8,128)S(1)}, s32[27,384]{1,0:T(8,128)}, u32[]{:S(2)}) copy-start(s32[27,384]{1,0:T(8,128)} %rule_ref.1) | copy-start | bytes 124420
  4.8 0.8 %copy-start.4 = (bf16[64,384]{1,0:T(8,128)(2,1)S(1)}, bf16[64,384]{1,0:T(8,128)(2,1)}, u32[]{:S(2)}) copy-start(bf16[64,384]{1,0:T(8,128)(2,1)} %cot_ref.1) | copy-start | bytes 147460

commit v2 on v1

--- a/solution.py
+++ b/solution.py
@@ -9,6 +9,7 @@
 from jax.sharding import PartitionSpec as P
 
 LANES = 128
+LIMIT_MIB = 60
 BF = jnp.bfloat16
 F32 = jnp.float32
 TRANS_RHS = (((1,), (1,)), ((), ()))
@@ -21,11 +22,42 @@
     return row_parts, col_parts, width // row_parts, piece_cols
 
 
+def piece_of(plan, j):
+    row_parts, col_parts, piece_rows, piece_cols = plan
+    r, c = (j // col_parts) * piece_rows, (j % col_parts) * piece_cols
+    return slice(r, r + piece_rows), slice(c, c + piece_cols)
+
+
+def finish(plan, out_near, dx_near, ag_near, out_far, dx_far, g1_far, g2_far, ag, g_ref, sem):
+    chips, cols = ag.shape[1], g_ref.shape[2]
+    loads = [pltpu.make_async_copy(ag_near.at[g], ag.at[g], sem.at[g]) for g in range(2)]
+    moves = [
+        pltpu.make_async_copy(out_near, out_far, sem.at[2]),
+        pltpu.make_async_copy(dx_near, dx_far, sem.at[3]),
+        pltpu.make_async_copy(g_ref.at[0], g1_far, sem.at[4]),
+        pltpu.make_async_copy(g_ref.at[1], g2_far, sem.at[5]),
+    ]
+    for copy in (loads[0], loads[1], moves[0], moves[1]):
+        copy.start()
+    for g in range(2):
+        loads[g].wait()
+        for j in range(chips):
+            r, c = piece_of(plan, j)
+            live = min(c.stop, cols) - c.start
+            if live > 0:
+                g_ref[g, r, c.start : c.start + live] = ag[g, j, :, :live].astype(F32)
+        moves[2 + g].start()
+    for copy in moves:
+        copy.wait()
+
+
 def kernel(
     count, plan, scale,
-    x_ref, rule_ref, lists_ref, w1_ref, w2_ref, cot_ref,
-    out_ref, dx_ref, g1_ref, g2_ref,
-    hot, gat_a, gat_b, mir1, mir2, own, hsend, halo, part, peer_in, rs_out, rs_in, ag,
+    x_hbm, rule_hbm, lists_hbm, w1_hbm, w2_hbm, cot_hbm,
+    out_hbm, dx_hbm, ag,
+    out_ref, dx_ref, mine, done_sem,
+    x_ref, rule_ref, lists_ref, w1_ref, w2_ref, cot_ref, in_sem,
+    hot, gat_a, gat_b, mir1, mir2, own, hsend, halo, part, peer_in, rs_out, rs_in,
     hs_sem, hr_sem, p_sem, rs_s, rs_r, ag_s, ag_r, fw_s, fw_r,
 ):
     width, rows = x_ref.shape
@@ -46,7 +78,22 @@
     def there(distance):
         return 2 * lax.rem(chip + distance, chips) + core
 
+    x_in, cot_in, lists_in, rule_in, w1_in, w2_in = (
+        pltpu.make_async_copy(far, near, in_sem.at[i])
+        for i, (far, near) in enumerate(
+            (
+                (x_hbm, x_ref),
+                (cot_hbm, cot_ref),
+                (lists_hbm, lists_ref),
+                (rule_hbm, rule_ref),
+                (w1_hbm, w1_ref),
+                (w2_hbm, w2_ref),
+            )
+        )
+    )
     barrier = pltpu.get_barrier_semaphore()
+    for fetch in (x_in, cot_in, lists_in, rule_in, w2_in, w1_in):
+        fetch.start()
     beside = lax.rem(t + 2 * core - 1 + count, count)
     pl.semaphore_signal(barrier, inc=1, device_id={"tile": peer})
     pl.semaphore_signal(barrier, inc=1, device_id={"tile": beside})
@@ -64,7 +111,7 @@
 
     def pick_boundary(phase):
         for up in range(2):
-            listed = jnp.broadcast_to(lists_ref[up : up + 1, :], (2 * width, LANES))
+            listed = jnp.broadcast_to(lists_ref[:, up : up + 1], (2 * width, LANES))
             chosen = jnp.zeros((2 * width, LANES), F32)
             for q in range(blocks):
                 chosen = jnp.where(listed == q, own[phase, q], chosen)
@@ -105,12 +152,15 @@
         def _():
             halo_copy(phase, 1).wait_send()
 
+    for fetch in (x_in, cot_in, lists_in):
+        fetch.wait()
     for q in range(blocks):
         own[0, q] = jnp.concatenate([x_ref[:, lanes(q)], cot_ref[:, lanes(q)]], axis=0).astype(F32)
     pick_boundary(0)
     pl.semaphore_wait(barrier, chips + 1)
     send_halo(0)
 
+    rule_in.wait()
     reach = jax.lax.broadcasted_iota(jnp.int32, (LANES, LANES), 0)
     firsts = {}
     for a in range(3):
@@ -132,6 +182,8 @@
                 hit = jnp.broadcast_to(row, (LANES, LANES)) == reach
                 hot[a, b, :, lanes(j)] = jnp.where(hit, 1.0, 0.0).astype(BF)
 
+    w2_in.wait()
+    w1_in.wait()
     for w_ref, m_ref in ((w2_ref, mir2), (w1_ref, mir1)):
         for k in range(0, offsets, 2):
             last = min(k + 2, offsets)
@@ -224,8 +276,7 @@
         gather(1, 1, b)
 
     def piece(j):
-        r, c = (j // col_parts) * piece_rows, (j % col_parts) * piece_cols
-        return slice(r, r + piece_rows), slice(c, c + piece_cols)
+        return piece_of(plan, j)
 
     to_peer.wait_recv()
     for j in range(chips):
@@ -263,18 +314,23 @@
     out_ref[...] = (second + x_ref[...].astype(F32)).astype(BF)
     d_input = jnp.dot(mir1[...], gat_b[...], preferred_element_type=F32)
     dx_ref[...] = (cot_ref[...].astype(F32) + d_input).astype(BF)
+    out_copy = pltpu.make_async_copy(out_ref, out_hbm, done_sem.at[0])
+    dx_copy = pltpu.make_async_copy(dx_ref, dx_hbm, done_sem.at[1])
+    out_copy.start()
+    dx_copy.start()
 
     total = rs_out[chip].astype(F32)
     for d in range(1, chips):
         source, arrival = rs_arrival(d)
         arrival.wait_recv()
         total = total + rs_in[source].astype(F32)
-    ag[core, chip] = (total * scale).astype(BF)
+    mine[...] = (total * scale).astype(BF)
+    keep = pltpu.make_async_copy(mine, ag.at[core, chip], done_sem.at[2])
 
     def ag_copy(d):
         target = lax.rem(chip + d, chips)
         return pltpu.make_async_remote_copy(
-            src_ref=ag.at[core, chip],
+            src_ref=mine,
             dst_ref=ag.at[core, chip],
             send_sem=ag_s.at[target],
             recv_sem=ag_r.at[chip],
@@ -283,16 +339,16 @@
 
     def ag_arrival(source):
         return pltpu.make_async_remote_copy(
-            src_ref=ag.at[core, source],
+            src_ref=mine,
             dst_ref=ag.at[core, source],
             send_sem=ag_s.at[source],
             recv_sem=ag_r.at[source],
             device_id={"tile": 2 * source + core},
         )
 
-    def forward(source):
-        return pltpu.make_async_remote_copy(
-            src_ref=ag.at[core, source],
+    def forward(source, held=None):
+        return pltpu.make_async_remote_copy(
+            src_ref=ag.at[core, source] if held is None else held,
             dst_ref=ag.at[core, source],
             send_sem=fw_s.at[source],
             recv_sem=fw_r.at[source],
@@ -310,21 +366,14 @@
 
     for d in range(1, chips):
         ag_copy(d).start()
-    forward(chip).start()
+    forward(chip, mine).start()
+    keep.start()
     for d in range(1, chips):
         source = lax.rem(chip + chips - d, chips)
         ag_arrival(source).wait_recv()
         forward(source).start()
     for j in range(chips):
         forwarded(j).wait_recv()
-    for j in range(chips):
-        r, c = piece(j)
-        live = min(c.stop, cols) - c.start
-        if live > 0:
-            place = slice(c.start, c.start + live)
-            g1_ref[r, place] = ag[0, j, :, :live].astype(F32)
-            g2_ref[r, place] = ag[1, j, :, :live].astype(F32)
-
     wait_sent(0)
     wait_sent(1)
     to_peer.wait_send()
@@ -333,6 +382,8 @@
         ag_copy(d).wait_send()
     for j in range(chips):
         forward(j).wait_send()
+    for copy in (out_copy, dx_copy, keep):
+        copy.wait()
 
 
 def body(count, features, rulebook, send_lists, weight_first, weight_second, cotangent):
@@ -345,18 +396,28 @@
     row_parts, col_parts, piece_rows, piece_cols = plan
     scale = 1.0 / math.sqrt(rows * count)
     dma = pltpu.SemaphoreType.DMA
-    vmem = pl.BlockSpec(memory_space=pltpu.VMEM)
-    return pl.pallas_call(
+    hbm = pl.BlockSpec(memory_space=pltpu.HBM)
+    results = pl.pallas_call(
         functools.partial(kernel, count, plan, scale),
         out_shape=(
             jax.ShapeDtypeStruct((width, rows), BF),
             jax.ShapeDtypeStruct((width, rows), BF),
-            jax.ShapeDtypeStruct((width, cols), F32),
-            jax.ShapeDtypeStruct((width, cols), F32),
+            jax.ShapeDtypeStruct((2, chips, piece_rows, piece_cols), BF),
         ),
-        in_specs=[vmem] * 6,
-        out_specs=(vmem,) * 4,
+        in_specs=[hbm] * 6,
+        out_specs=(hbm,) * 3,
         scratch_shapes=[
+            pltpu.VMEM((width, rows), BF),
+            pltpu.VMEM((width, rows), BF),
+            pltpu.VMEM((piece_rows, piece_cols), BF),
+            dma((3,)),
+            pltpu.VMEM((width, rows), BF),
+            pltpu.VMEM((offsets, rows), jnp.int32),
+            pltpu.VMEM((1, 2), jnp.int32),
+            pltpu.VMEM((width, cols), BF),
+            pltpu.VMEM((width, cols), BF),
+            pltpu.VMEM((width, rows), BF),
+            dma((6,)),
             pltpu.VMEM((3, blocks, LANES, offsets // 3 * LANES), BF),
             pltpu.VMEM((cols, rows), BF),
             pltpu.VMEM((cols, rows), BF),
@@ -369,7 +430,6 @@
             pltpu.VMEM((width, col_parts * piece_cols), F32),
             pltpu.VMEM((chips, piece_rows, piece_cols), BF),
             pltpu.VMEM((chips, piece_rows, piece_cols), BF),
-            pltpu.VMEM((2, chips, piece_rows, piece_cols), BF),
             dma((2, 2)),
             dma((2, 2)),
             dma((2,)),
@@ -381,9 +441,26 @@
             dma((chips,)),
         ],
         compiler_params=pltpu.CompilerParams(
-            collective_id=0, has_side_effects=True, vmem_limit_bytes=40 * 1024 * 1024
+            collective_id=0, has_side_effects=True, vmem_limit_bytes=LIMIT_MIB * 1024 * 1024
         ),
-    )(features, rulebook, send_lists, weight_first, weight_second, cotangent)
+    )(features, rulebook, send_lists.T, weight_first, weight_second, cotangent)
+    return pl.pallas_call(
+        functools.partial(finish, plan),
+        out_shape=(
+            jax.ShapeDtypeStruct((width, rows), BF),
+            jax.ShapeDtypeStruct((width, rows), BF),
+            jax.ShapeDtypeStruct((width, cols), F32),
+            jax.ShapeDtypeStruct((width, cols), F32),
+        ),
+        in_specs=[hbm] * 3,
+        out_specs=(hbm,) * 4,
+        scratch_shapes=[
+            pltpu.VMEM((2, chips, piece_rows, piece_cols), BF),
+            pltpu.VMEM((2, width, cols), F32),
+            dma((6,)),
+        ],
+        compiler_params=pltpu.CompilerParams(vmem_limit_bytes=LIMIT_MIB * 1024 * 1024),
+    )(*results)
 
 
 def solution(mesh):

time: 34 us -> 30.8 us (0.906)
  local copies, waits for them, and re-layouts: 7.79 us -> 0 us
  Pallas kernels: 25.2 us -> 30 us
    unnamed x15 -> x0, local copies, waits for them, and re-layouts: 7.79 us -> none
    pallas_call x0 -> x1, Pallas kernels: none -> 4.14 us  [body(): pl.pallas_call(functools.partial(finish, plan), out_shape=(jax.ShapeDtype...]
    pallas_call x1, Pallas kernels: 25.2 us -> 25.8 us  [body(): pl.pallas_call(functools.partial(kernel, count, plan, scale), out_shape=(...]
where the time goes in v2:
time: 30.8 us; the launch traced here: 30.6 us
  Pallas kernels  30 us (97%)
  between operations  0.64 us (2%)
    pallas_call x1, Pallas kernels, body(): pl.pallas_call(functools.partial(kernel, count, plan, scale), out_shape=(...  25.8 us
    pallas_call x1, Pallas kernels, body(): pl.pallas_call(functools.partial(finish, plan), out_shape=(jax.ShapeDtype...  4.14 us

profile of v2, /device:TPU:0, one launch (start us, length us, event | category | flops | bytes accessed | tf_op | source)
XLA Modules:
  0.0 30.6 jit_solution(16240952467282066699)
XLA Ops:
  0.6 25.8 %shard_map.93 = (bf16[64,384]{1,0:T(8,128)(2,1)}, bf16[64,384]{1,0:T(8,128)(2,1)}, bf16[2,8,16,896]{3,2,1,0:T(8,128)(2,1)}) custom-call(bf16[64,384]{1,0:T(8,128)(2,1)} %x_hbm.1, s32[27,384]{1,0:T(8,128)} %rule_hbm.1, s32[1,2]{1,0:T(1,128)} %bitcast.1, bf16[64,1728]{1,0:T(8,128)(2,1)} %w1_hbm.1, bf16[64,1728]{1,0:T(8,128)(2,1)} %w2_hbm.1, ...), custom_call_target="tpu_custom_call" | custom-call | tf_op jit(solution)/shard_map/pallas_call | solution.py:400
  26.5 4.1 %shard_map.94 = (bf16[64,384]{1,0:T(8,128)(2,1)}, bf16[64,384]{1,0:T(8,128)(2,1)}, f32[64,1728]{1,0:T(8,128)}, f32[64,1728]{1,0:T(8,128)}) custom-call(bf16[64,384]{1,0:T(8,128)(2,1)} %get-tuple-element.7.out_near, bf16[64,384]{1,0:T(8,128)(2,1)} %get-tuple-element.8.dx_near, bf16[2,8,16,896]{3,2,1,0:T(8,128)(2,1)} %get-tuple-element.9.ag_near), custom_call_target="tpu_custom_call" | custom-call | tf_op jit(solution)/shard_map/pallas_call | solution.py:447
